TPU v7x, 32 devices: a whole 2x2x4 slice. The times are simulated.
32 devices in a mesh: replica: 2 (over y), node: 16 (over z, x, core).
Axes of the slice: x: 2, y: 2, z: 4, core: 2. Of those that a mesh axis runs over, the one named last changes fastest.
Arguments:
- x_rows: bfloat16 [4096, 2048], P(('replica', 'node')), parts along dimension 0, may hold values from -6 to 6
- out_grad: bfloat16 [4096, 2048], P(('replica', 'node')), parts along dimension 0, may hold values from -3 to 3
- expert_ids: int32 [4096, 4], P(('replica', 'node')), parts along dimension 0, may hold values from 0 to 7, all different within a row; in each aligned block of 128 rows (0 to 127, 128 to 255, ...) at most 80 rows name the same one
- gate_values: float32 [4096, 4], P(('replica', 'node')), parts along dimension 0, may hold values from 0.1 to 1
- w_gate: bfloat16 [16, 2048, 384], P('node'), may hold values from -0.125 to 0.125
- w_up: bfloat16 [16, 2048, 384], P('node'), may hold values from -0.125 to 0.125
- w_down: bfloat16 [16, 384, 2048], P('node'), may hold values from -0.21875 to 0.21875
Outputs:
- x_grad: bfloat16 [4096, 2048], P(('replica', 'node')), parts along dimension 0
- gate_grad: float32 [4096, 4], P(('replica', 'node')), parts along dimension 0
- grad_gate: bfloat16 [32, 2048, 384], P(('replica', 'node')), parts along dimension 0
- grad_up: bfloat16 [32, 2048, 384], P(('replica', 'node')), parts along dimension 0
- grad_down: bfloat16 [32, 384, 2048], P(('replica', 'node')), parts along dimension 0
There are 2 independent parts, one for each index of `replica`. A program takes and returns all parts, laid end to end along the dimension named above; an argument that names none is the same for every part. Nothing has to cross between parts.
Inputs may be any that keep to these rules, and one draw needn't show every extreme that they name: `expert_ids`: each row names 4 different experts; within the rows of one device no expert is named more than 80 times, and in some device's rows some expert exactly 80 times.
All inputs are finite; a program needn't handle non-finite values.
Results may differ from a plain program's by a relative error of at most 0.0063.
Values may be sent and summed in bfloat16 or wider, within the bound.
A program may use at most 128 MiB of HBM per device.

v0:
```python
import functools

import jax
import jax.numpy as jnp
from jax import lax
from jax.experimental import pallas as pl
from jax.experimental.pallas import tpu as pltpu
from jax.sharding import PartitionSpec as P


RING_NODES = 16


def partner(value, axis, bit):
    mask = 2**bit
    pairs = [(source, source ^ mask) for source in range(lax.axis_size(axis))]
    return lax.ppermute(value, axis, pairs)


def expert_backward(rows_in, rows_grad, rows_gate, gate_mat, up_mat, down_mat):
    contract_rows = (((0,), (0,)), ((), ()))
    contract_cols = (((1,), (1,)), ((), ()))
    pre_gate = jnp.dot(rows_in, gate_mat, preferred_element_type=jnp.float32)
    pre_up = jnp.dot(rows_in, up_mat, preferred_element_type=jnp.float32)
    sigmoid_gate = jax.nn.sigmoid(pre_gate)
    activation = pre_gate * sigmoid_gate
    hidden = (activation * pre_up).astype(jnp.bfloat16)
    upstream = lax.dot_general(
        rows_grad, down_mat, contract_cols, preferred_element_type=jnp.float32
    )
    gate_part = jnp.sum(hidden.astype(jnp.float32) * upstream, axis=1)
    grad_hidden = rows_gate[:, None] * upstream
    grad_pre_gate = (
        grad_hidden * pre_up * sigmoid_gate * (1.0 + pre_gate * (1.0 - sigmoid_gate))
    ).astype(jnp.bfloat16)
    grad_pre_up = (grad_hidden * activation).astype(jnp.bfloat16)
    scaled_grad = (rows_gate[:, None] * rows_grad.astype(jnp.float32)).astype(jnp.bfloat16)
    down_grad = lax.dot_general(
        hidden, scaled_grad, contract_rows, preferred_element_type=jnp.float32
    ).astype(jnp.bfloat16)
    gate_mat_grad = lax.dot_general(
        rows_in, grad_pre_gate, contract_rows, preferred_element_type=jnp.float32
    ).astype(jnp.bfloat16)
    up_mat_grad = lax.dot_general(
        rows_in, grad_pre_up, contract_rows, preferred_element_type=jnp.float32
    ).astype(jnp.bfloat16)
    input_part = lax.dot_general(
        grad_pre_gate, gate_mat, contract_cols, preferred_element_type=jnp.float32
    )
    input_part = input_part + lax.dot_general(
        grad_pre_up, up_mat, contract_cols, preferred_element_type=jnp.float32
    )
    return (gate_mat_grad, up_mat_grad, down_grad, input_part, gate_part)


def exchange_local(x_rows, out_grad, expert_ids, gate_values, w_gate, w_up, w_down):
    nodes = lax.axis_size("node")
    experts = nodes // 2
    tok_rows, width = x_rows.shape
    top_count = expert_ids.shape[1]
    capacity = 2 * max(1, 5 * tok_rows * top_count // (8 * experts))
    half_cap = capacity // 2
    flat_ids = expert_ids.reshape(-1)
    one_hot = (flat_ids[:, None] == jnp.arange(experts, dtype=jnp.int32)[None, :]).astype(jnp.int32)
    earlier = jnp.cumsum(one_hot, axis=0) - one_hot
    slot_index = jnp.sum(earlier * one_hot, axis=1)
    send_place = flat_ids * capacity + slot_index
    send_in = (
        jnp.zeros((experts * capacity, width), jnp.bfloat16)
        .at[send_place]
        .set(jnp.repeat(x_rows, top_count, axis=0))
    )
    send_grad = (
        jnp.zeros((experts * capacity, width), jnp.bfloat16)
        .at[send_place]
        .set(jnp.repeat(out_grad, top_count, axis=0))
    )
    send_gate = (
        jnp.zeros((experts * capacity,), jnp.bfloat16)
        .at[send_place]
        .set(gate_values.reshape(-1).astype(jnp.bfloat16))
    )
    gate_mat = w_gate[0]
    up_mat = w_up[0]
    down_mat = w_down[0]
    mine_in, mine_grad, mine_gate = (
        lax.all_to_all(
            send_in.reshape(nodes, half_cap, width), "node", split_axis=0, concat_axis=0, tiled=True
        ),
        lax.all_to_all(
            send_grad.reshape(nodes, half_cap, width),
            "node",
            split_axis=0,
            concat_axis=0,
            tiled=True,
        ),
        lax.all_to_all(
            send_gate.reshape(nodes, half_cap), "node", split_axis=0, concat_axis=0, tiled=True
        ),
    )
    other_in, other_grad, other_gate = partner((mine_in, mine_grad, mine_gate), "node", 0)
    rows_in = jnp.concatenate([mine_in, other_in], axis=1).reshape(-1, width)
    rows_grad = jnp.concatenate([mine_grad, other_grad], axis=1).reshape(-1, width)
    rows_gate = jnp.concatenate([mine_gate, other_gate], axis=1).reshape(-1).astype(jnp.float32)
    gate_mat_grad, up_mat_grad, down_grad, input_part, gate_part = expert_backward(
        rows_in, rows_grad, rows_gate, gate_mat, up_mat, down_mat
    )
    input_part = input_part.reshape(nodes, capacity, width)
    gate_part = gate_part.reshape(nodes, capacity)
    partner_input, partner_gate = partner(
        (input_part[:, half_cap:], gate_part[:, half_cap:]), "node", 0
    )
    own_input = input_part[:, :half_cap] + partner_input
    own_gate = gate_part[:, :half_cap] + partner_gate
    back_input, back_gate = (
        lax.all_to_all(own_input, "node", split_axis=0, concat_axis=0, tiled=True),
        lax.all_to_all(own_gate, "node", split_axis=0, concat_axis=0, tiled=True),
    )
    summed_input = back_input.reshape(-1, width)
    summed_gate = back_gate.reshape(-1)
    x_grad = (
        summed_input[send_place]
        .reshape(tok_rows, top_count, width)
        .sum(axis=1)
        .astype(jnp.bfloat16)
    )
    gate_grad = summed_gate[send_place].reshape(tok_rows, top_count)
    return (x_grad, gate_grad, gate_mat_grad[None], up_mat_grad[None], down_grad[None])


def ring_kernel(
    nodes,
    x_hbm,
    g_hbm,
    gt_hbm,
    wg_hbm,
    wu_hbm,
    wd_hbm,
    dx_hbm,
    gg_hbm,
    dwg_hbm,
    dwu_hbm,
    dwd_hbm,
    tok,
    gates,
    w_mat,
    wd_mat,
    acc_in,
    acc_down,
    upstream,
    grad_pre,
    hidden,
    gate_col,
    gate_part,
    dx_part,
    home,
    ring_sum,
    side_recv,
    side_send,
    ring_gate,
    side_gate_recv,
    side_gate_send,
    gate_rows,
    home_gate,
    dx_out,
    load_sem,
    tok_ring_send,
    tok_ring_recv,
    tok_side_send,
    tok_side_recv,
    gates_ring_send,
    gates_ring_recv,
    gates_side_send,
    gates_side_recv,
    sum_ring_send,
    sum_ring_recv,
    sum_side_send,
    sum_side_recv,
    gsum_ring_send,
    gsum_ring_recv,
    gsum_side_send,
    gsum_side_recv,
):
    chips = nodes // 2
    depth = chips // 2
    rows, width = x_hbm.shape
    lanes = 128
    tiles = wg_hbm.shape[2] // lanes
    cols = 512
    me = lax.axis_index("node")
    core = me % 2
    mate = 1 - core
    chip = me // 2
    side = chip % 2
    place = chip // 2 + side * (2 * depth - 1 - 2 * (chip // 2))

    def node_at(where):
        where = (where + chips) % chips
        row = where // depth
        level = where + row * (2 * depth - 1 - 2 * where)
        return (level * 2 + row) * 2 + core

    step_dir = 1 - 2 * core
    ahead = {"node": node_at(place + step_dir)}
    behind = {"node": node_at(place - step_dir)}
    other = {"node": chip * 2 + mate}

    loads = [
        (x_hbm, tok.at[0, 0, core]),
        (g_hbm, tok.at[0, 1, core]),
        (gt_hbm, gates.at[0, core]),
        (wd_hbm.at[0], wd_mat),
    ]
    for j in range(tiles):
        part = pl.ds(j * lanes, lanes)
        loads.append((wg_hbm.at[0, :, part], w_mat.at[j, :, pl.ds(0, lanes)]))
        loads.append((wu_hbm.at[0, :, part], w_mat.at[j, :, pl.ds(lanes, lanes)]))
    loads = [
        pltpu.make_async_copy(source, target, load_sem.at[i])
        for i, (source, target) in enumerate(loads)
    ]
    for load in loads:
        load.start()

    barrier = pltpu.get_barrier_semaphore()
    for target in (ahead, behind, other):
        pl.semaphore_signal(barrier, inc=1, device_id=target, device_id_type=pl.DeviceIdType.MESH)
    pl.semaphore_wait(barrier, 3)

    def remote(source, target, send, recv, device):
        return pltpu.make_async_remote_copy(
            src_ref=source,
            dst_ref=target,
            send_sem=send,
            recv_sem=recv,
            device_id=device,
            device_id_type=pl.DeviceIdType.MESH,
        )

    def tok_ring(s):
        return (
            remote(
                tok.at[s, :, core],
                tok.at[s + 1, :, core],
                tok_ring_send.at[s],
                tok_ring_recv.at[s + 1],
                ahead,
            ),
            remote(
                gates.at[s, core],
                gates.at[s + 1, core],
                gates_ring_send.at[s],
                gates_ring_recv.at[s + 1],
                ahead,
            ),
        )

    def tok_side(s, whose):
        return (
            remote(
                tok.at[s, :, whose],
                tok.at[s, :, whose],
                tok_side_send.at[s],
                tok_side_recv.at[s],
                other,
            ),
            remote(
                gates.at[s, whose],
                gates.at[s, whose],
                gates_side_send.at[s],
                gates_side_recv.at[s],
                other,
            ),
        )

    def sum_ring(s):
        return (
            remote(
                ring_sum.at[s],
                ring_sum.at[s + 1],
                sum_ring_send.at[s],
                sum_ring_recv.at[s + 1],
                ahead,
            ),
            remote(
                ring_gate.at[s],
                ring_gate.at[s + 1],
                gsum_ring_send.at[s],
                gsum_ring_recv.at[s + 1],
                ahead,
            ),
        )

    def sum_side(s):
        return (
            remote(
                side_send.at[s], side_recv.at[s], sum_side_send.at[s], sum_side_recv.at[s], other
            ),
            remote(
                side_gate_send.at[s],
                side_gate_recv.at[s],
                gsum_side_send.at[s],
                gsum_side_recv.at[s],
                other,
            ),
        )

    for load in loads[:3]:
        load.wait()

    acc_in[...] = jnp.zeros_like(acc_in)
    acc_down[...] = jnp.zeros_like(acc_down)
    contract_last = (((1,), (1,)), ((), ()))
    contract_first = (((0,), (0,)), ((), ()))
    slots = gates.shape[2]

    def step(s, carry):
        @pl.when(s >= 1)
        def _():
            for copy in tok_ring(s - 1):
                copy.wait_recv()

        @pl.when(s < chips - 1)
        def _():
            for copy in tok_ring(s):
                copy.start()

        for copy in tok_side(s, core):
            copy.start()

        @pl.when(s == 0)
        def _():
            for load in loads[3:]:
                load.wait()

        for copy in tok_side(s, mate):
            copy.wait_recv()

        pick = (lax.broadcasted_iota(jnp.int32, (slots, lanes), 0) == chip).astype(jnp.bfloat16)
        for c in range(2):
            gate_col[c * rows : (c + 1) * rows, :] = lax.dot_general(
                gates[s, c], pick, contract_first, preferred_element_type=jnp.float32
            )
        gate = gate_col[...]

        up = lax.dot_general(
            tok[s, 1].reshape(2 * rows, width),
            wd_mat[...],
            contract_last,
            preferred_element_type=jnp.float32,
        )
        for j in range(tiles):
            upstream[j] = up[:, j * lanes : (j + 1) * lanes]
        gate_part[...] = jnp.zeros_like(gate_part)

        @pl.loop(0, tiles)
        def _(j):
            pre = jnp.dot(
                tok[s, 0].reshape(2 * rows, width), w_mat[j], preferred_element_type=jnp.float32
            )
            pre_gate, pre_up = pre[:, :lanes], pre[:, lanes:]
            sig = jax.nn.sigmoid(pre_gate)
            act = pre_gate * sig
            hid = (act * pre_up).astype(jnp.bfloat16)
            ups = upstream[j]
            gate_part[...] += hid.astype(jnp.float32) * ups
            grad_hidden = gate_col[...] * ups
            grad_pre[j, :, :lanes] = (
                grad_hidden * pre_up * sig * (1.0 + pre_gate * (1.0 - sig))
            ).astype(jnp.bfloat16)
            grad_pre[j, :, lanes:] = (grad_hidden * act).astype(jnp.bfloat16)
            hidden[j] = hid

        @pl.loop(0, width // cols)
        def _(n):
            at = pl.ds(pl.multiple_of(n * cols, cols), cols)
            total = None
            for j in range(tiles):
                term = lax.dot_general(
                    grad_pre[j], w_mat[j, at, :], contract_last, preferred_element_type=jnp.float32
                )
                total = term if total is None else total + term
            dx_part[0, :, at] = total[:rows]
            dx_part[1, :, at] = total[rows:]

        for c in range(2):
            column = jnp.sum(gate_part[c * rows : (c + 1) * rows, :], axis=1, keepdims=True)
            across = jnp.transpose(jnp.broadcast_to(column, (rows, lanes)))[:slots]
            mine = lax.broadcasted_iota(jnp.int32, (slots, rows), 0) == chip
            gate_rows[c] = jnp.where(mine, across, 0.0)

        side_send[s] = dx_part[mate].astype(jnp.bfloat16)
        side_gate_send[s] = gate_rows[mate]
        for copy in sum_side(s):
            copy.start()
        for copy in sum_side(s):
            copy.wait_recv()

        @pl.when(s == 0)
        def _():
            home[...] = dx_part[core] + side_recv[s].astype(jnp.float32)
            home_gate[...] = gate_rows[core] + side_gate_recv[s]

        @pl.when(s == 1)
        def _():
            ring_sum[s] = (dx_part[core] + side_recv[s].astype(jnp.float32)).astype(jnp.bfloat16)
            ring_gate[s] = gate_rows[core] + side_gate_recv[s]

        @pl.when(s >= 2)
        def _():
            for copy in sum_ring(s - 1):
                copy.wait_recv()
            ring_sum[s] = (
                dx_part[core]
                + side_recv[s].astype(jnp.float32)
                + ring_sum[s].astype(jnp.float32)
            ).astype(jnp.bfloat16)
            ring_gate[s] = gate_rows[core] + side_gate_recv[s] + ring_gate[s]

        @pl.when(s >= 1)
        def _():
            for copy in sum_ring(s):
                copy.start()

        @pl.loop(0, width // cols)
        def _(n):
            at = pl.ds(pl.multiple_of(n * cols, cols), cols)
            x_tile = tok[s, 0, :, :, at].reshape(2 * rows, cols)
            g_tile = tok[s, 1, :, :, at].reshape(2 * rows, cols).astype(jnp.float32)
            scaled = jnp.concatenate(
                [
                    (g_tile[:, k * lanes : (k + 1) * lanes] * gate_col[...]).astype(jnp.bfloat16)
                    for k in range(cols // lanes)
                ],
                axis=1,
            )
            for j in range(tiles):
                acc_in[j, at, :] += lax.dot_general(
                    x_tile, grad_pre[j], contract_first, preferred_element_type=jnp.float32
                )
                acc_down[j, :, at] += lax.dot_general(
                    hidden[j], scaled, contract_first, preferred_element_type=jnp.float32
                )

        return carry

    lax.fori_loop(0, chips, step, 0)

    for j in range(tiles):
        w_mat[j] = acc_in[j].astype(jnp.bfloat16)
        wd_mat[j * lanes : (j + 1) * lanes, :] = acc_down[j].astype(jnp.bfloat16)
    stores = [(wd_mat, dwd_hbm.at[0])]
    for j in range(tiles):
        part = pl.ds(j * lanes, lanes)
        stores.append((w_mat.at[j, :, pl.ds(0, lanes)], dwg_hbm.at[0, :, part]))
        stores.append((w_mat.at[j, :, pl.ds(lanes, lanes)], dwu_hbm.at[0, :, part]))
    stores = [
        pltpu.make_async_copy(source, target, load_sem.at[i])
        for i, (source, target) in enumerate(stores)
    ]
    for store in stores:
        store.start()

    for copy in sum_ring(chips - 1):
        copy.wait_recv()
    dx_out[...] = (home[...] + ring_sum[chips].astype(jnp.float32)).astype(jnp.bfloat16)
    home_gate[...] += ring_gate[chips]
    last = [
        pltpu.make_async_copy(dx_out, dx_hbm, load_sem.at[len(stores)]),
        pltpu.make_async_copy(home_gate, gg_hbm, load_sem.at[len(stores) + 1]),
    ]
    for store in last:
        store.start()

    def drain(s, carry):
        @pl.when(s < chips - 1)
        def _():
            for copy in tok_ring(s):
                copy.wait_send()

        @pl.when(s >= 1)
        def _():
            for copy in sum_ring(s):
                copy.wait_send()

        for copy in tok_side(s, core):
            copy.wait_send()
        for copy in sum_side(s):
            copy.wait_send()
        return carry

    lax.fori_loop(0, chips, drain, 0)
    for store in stores + last:
        store.wait()


def ring_local(x_rows, out_grad, expert_ids, gate_values, w_gate, w_up, w_down):
    nodes = lax.axis_size("node")
    chips = nodes // 2
    rows, width = x_rows.shape
    hid = w_gate.shape[2]
    lanes = 128
    tiles = hid // lanes
    slots = (chips + 15) // 16 * 16
    expert = jnp.arange(slots, dtype=jnp.int32)[:, None]
    named = [expert == expert_ids[:, k][None, :] for k in range(expert_ids.shape[1])]
    gate_table = sum(
        jnp.where(named[k], gate_values[:, k][None, :], 0.0) for k in range(len(named))
    ).astype(jnp.bfloat16)
    any_space = pl.BlockSpec(memory_space=pl.ANY)
    bf16, f32 = jnp.bfloat16, jnp.float32
    dma = pltpu.SemaphoreType.DMA
    flops = 2 * nodes * rows * width * hid * 8
    x_grad, gate_sum, d_gate, d_up, d_down = pl.pallas_call(
        functools.partial(ring_kernel, nodes),
        out_shape=(
            jax.ShapeDtypeStruct((rows, width), bf16),
            jax.ShapeDtypeStruct((slots, rows), f32),
            jax.ShapeDtypeStruct((1, width, hid), bf16),
            jax.ShapeDtypeStruct((1, width, hid), bf16),
            jax.ShapeDtypeStruct((1, hid, width), bf16),
        ),
        in_specs=[any_space] * 6,
        out_specs=(any_space,) * 5,
        scratch_shapes=[
            pltpu.VMEM((chips, 2, 2, rows, width), bf16),
            pltpu.VMEM((chips, 2, slots, rows), bf16),
            pltpu.VMEM((tiles, width, 2 * lanes), bf16),
            pltpu.VMEM((hid, width), bf16),
            pltpu.VMEM((tiles, width, 2 * lanes), f32),
            pltpu.VMEM((tiles, lanes, width), f32),
            pltpu.VMEM((tiles, 2 * rows, lanes), f32),
            pltpu.VMEM((tiles, 2 * rows, 2 * lanes), bf16),
            pltpu.VMEM((tiles, 2 * rows, lanes), bf16),
            pltpu.VMEM((2 * rows, lanes), f32),
            pltpu.VMEM((2 * rows, lanes), f32),
            pltpu.VMEM((2, rows, width), f32),
            pltpu.VMEM((rows, width), f32),
            pltpu.VMEM((chips + 1, rows, width), bf16),
            pltpu.VMEM((chips, rows, width), bf16),
            pltpu.VMEM((chips, rows, width), bf16),
            pltpu.VMEM((chips + 1, slots, rows), f32),
            pltpu.VMEM((chips, slots, rows), f32),
            pltpu.VMEM((chips, slots, rows), f32),
            pltpu.VMEM((2, slots, rows), f32),
            pltpu.VMEM((slots, rows), f32),
            pltpu.VMEM((rows, width), bf16),
            dma((4 + 2 * tiles,)),
        ]
        + [dma((chips + 1,))] * 16,
        compiler_params=pltpu.CompilerParams(
            collective_id=0, has_side_effects=True, vmem_limit_bytes=60 * 2**20
        ),
        cost_estimate=pl.CostEstimate(
            flops=flops, bytes_accessed=12 * width * hid, transcendentals=nodes * rows * hid
        ),
    )(x_rows, out_grad, gate_table, w_gate, w_up, w_down)
    gate_grad = jnp.stack(
        [jnp.sum(jnp.where(chosen, gate_sum, 0.0), axis=0) for chosen in named], axis=1
    )
    return (x_grad, gate_grad, d_gate, d_up, d_down)


def solution(mesh):
    local = ring_local if mesh.shape["node"] <= RING_NODES else exchange_local
    return jax.shard_map(
        local,
        mesh=mesh,
        in_specs=(
            P(("replica", "node"), None),
            P(("replica", "node"), None),
            P(("replica", "node"), None),
            P(("replica", "node"), None),
            P("node", None, None),
            P("node", None, None),
            P("node", None, None),
        ),
        out_specs=(
            P(("replica", "node"), None),
            P(("replica", "node"), None),
            P(("replica", "node"), None, None),
            P(("replica", "node"), None, None),
            P(("replica", "node"), None, None),
        ),
        check_vma=False,
    )
```

profile of v0, /device:TPU:0, one launch (start us, length us, event | category | flops | bytes accessed | tf_op | source)
XLA Modules:
  0.0 148.6 jit_solution(17350004164890692254)
XLA Ops:
  0.6 0.8 slice_bitcast_fusion.7
  1.5 0.8 slice_bitcast_fusion.6
  2.3 0.6 add_convert_fusion.gt_hbm
  2.9 136.5 %shard_map.110 = (bf16[128,2048]{1,0:T(8,128)(2,1)}, f32[16,128]{1,0:T(8,128)}, bf16[1,2048,384]{2,1,0:T(8,128)(2,1)}, bf16[1,2048,384]{2,1,0:T(8,128)(2,1)}, bf16[1,384,2048]{2,1,0:T(8,128)(2,1)}) custom-call(bf16[128,2048]{1,0:T(8,128)(2,1)} %x_hbm.1, bf16[128,2048]{1,0:T(8,128)(2,1)} %g_hbm.1, bf16[16,128]{1,0:T(8,128)(2,1)} %add_convert_fusion.gt_hbm, ...), custom_call_target="tpu_custom_call" | custom-call | flops 25769803776 | bytes 9437184 | tf_op jit(solution)/shard_map/pallas_call | solution.py:514
  139.4 0.7 select_reduce_fusion.3
  140.1 0.6 pad_maximum_fusion
  140.7 1.9 %copy.16 = bf16[128,2048]{1,0:T(8,128)(2,1)} copy(bf16[128,2048]{1,0:T(8,128)(2,1)} %get-tuple-element.32) | data formatting | bytes 1048576
  142.6 0.0 copy-start.1
  142.6 2.8 %copy.17 = bf16[1,2048,384]{2,1,0:T(8,128)(2,1)} copy(bf16[1,2048,384]{2,1,0:T(8,128)(2,1)} %get-tuple-element.34) | data formatting | bytes 3145728
  145.4 0.0 copy-done.1
  145.4 0.0 copy-start
  145.4 1.1 copy.18
  146.6 0.8 copy-done
  147.4 1.1 copy.19
Async XLA Ops:
  142.6 2.8 %copy-start.1 = (bf16[1,2048,384]{2,1,0:T(8,128)(2,1)S(1)}, bf16[1,2048,384]{2,1,0:T(8,128)(2,1)}, u32[]{:S(2)}) copy-start(bf16[1,2048,384]{2,1,0:T(8,128)(2,1)} %get-tuple-element.35) | copy-start | bytes 4718596
  145.4 2.0 %copy-start = (bf16[1,384,2048]{2,1,0:T(8,128)(2,1)S(1)}, bf16[1,384,2048]{2,1,0:T(8,128)(2,1)}, u32[]{:S(2)}) copy-start(bf16[1,384,2048]{2,1,0:T(8,128)(2,1)} %get-tuple-element.36) | copy-start | bytes 4718596
where the time goes:
time: 149 us
  Pallas kernels  137 us (92%)
  local copies, waits for them, and re-layouts  9.49 us (6%)
  other arithmetic  1.91 us (1%)
    pallas_call x1, Pallas kernels, ring_local(): pl.pallas_call(functools.partial(ring_kernel, nodes), out_shape=(jax.Shap...  137 us
    unnamed x8, local copies, waits for them, and re-layouts  7.83 us

commit v1 on v0

--- a/solution.py
+++ b/solution.py
@@ -154,6 +154,8 @@
     gate_part,
     dx_part,
     home,
+    own_part,
+    own_gate,
     ring_sum,
     side_recv,
     side_send,
@@ -237,58 +239,60 @@
             device_id_type=pl.DeviceIdType.MESH,
         )
 
-    def tok_ring(s):
-        return (
-            remote(
-                tok.at[s, :, core],
-                tok.at[s + 1, :, core],
-                tok_ring_send.at[s],
-                tok_ring_recv.at[s + 1],
-                ahead,
-            ),
-            remote(
-                gates.at[s, core],
-                gates.at[s + 1, core],
-                gates_ring_send.at[s],
-                gates_ring_recv.at[s + 1],
-                ahead,
-            ),
-        )
-
-    def tok_side(s, whose):
-        return (
-            remote(
-                tok.at[s, :, whose],
-                tok.at[s, :, whose],
-                tok_side_send.at[s],
-                tok_side_recv.at[s],
-                other,
-            ),
-            remote(
-                gates.at[s, whose],
-                gates.at[s, whose],
-                gates_side_send.at[s],
-                gates_side_recv.at[s],
-                other,
-            ),
-        )
-
-    def sum_ring(s):
-        return (
-            remote(
-                ring_sum.at[s],
-                ring_sum.at[s + 1],
-                sum_ring_send.at[s],
-                sum_ring_recv.at[s + 1],
-                ahead,
-            ),
-            remote(
-                ring_gate.at[s],
-                ring_gate.at[s + 1],
-                gsum_ring_send.at[s],
-                gsum_ring_recv.at[s + 1],
-                ahead,
-            ),
+    def tok_ring(s, kind):
+        return remote(
+            tok.at[s, kind, core],
+            tok.at[s + 1, kind, core],
+            tok_ring_send.at[s, kind],
+            tok_ring_recv.at[s + 1, kind],
+            ahead,
+        )
+
+    def gates_ring(s):
+        return remote(
+            gates.at[s, core],
+            gates.at[s + 1, core],
+            gates_ring_send.at[s],
+            gates_ring_recv.at[s + 1],
+            ahead,
+        )
+
+    def tok_side(s, kind, whose):
+        return remote(
+            tok.at[s, kind, whose],
+            tok.at[s, kind, whose],
+            tok_side_send.at[s, kind],
+            tok_side_recv.at[s, kind],
+            other,
+        )
+
+    def gates_side(s, whose):
+        return remote(
+            gates.at[s, whose],
+            gates.at[s, whose],
+            gates_side_send.at[s],
+            gates_side_recv.at[s],
+            other,
+        )
+
+    half = width // 2
+
+    def sum_ring(s, h):
+        return remote(
+            ring_sum.at[s, h],
+            ring_sum.at[s + 1, h],
+            sum_ring_send.at[s, h],
+            sum_ring_recv.at[s + 1, h],
+            ahead,
+        )
+
+    def gsum_ring(s):
+        return remote(
+            ring_gate.at[s],
+            ring_gate.at[s + 1],
+            gsum_ring_send.at[s],
+            gsum_ring_recv.at[s + 1],
+            ahead,
         )
 
     def sum_side(s):
@@ -308,33 +312,84 @@
     for load in loads[:3]:
         load.wait()
 
-    acc_in[...] = jnp.zeros_like(acc_in)
-    acc_down[...] = jnp.zeros_like(acc_down)
     contract_last = (((1,), (1,)), ((), ()))
     contract_first = (((0,), (0,)), ((), ()))
     slots = gates.shape[2]
 
+    lag = 2
+    kept = own_part.shape[0]
+
+    def add_and_send(s):
+        for copy in sum_side(s):
+            copy.wait_recv()
+        gates_total = own_gate[s % kept] + side_gate_recv[s]
+
+        @pl.when(s == 1)
+        def _():
+            ring_gate[s] = gates_total
+
+        @pl.when(s >= 2)
+        def _():
+            gsum_ring(s - 1).wait_recv()
+            ring_gate[s] = gates_total + ring_gate[s]
+
+        gsum_ring(s).start()
+        for h in range(2):
+            part = slice(h * half, (h + 1) * half)
+
+            @pl.when(s == 1)
+            def _():
+                ring_sum[s, h] = (
+                    own_part[s % kept, h] + side_recv[s, :, part].astype(jnp.float32)
+                ).astype(jnp.bfloat16)
+
+            @pl.when(s >= 2)
+            def _():
+                sum_ring(s - 1, h).wait_recv()
+                ring_sum[s, h] = (
+                    own_part[s % kept, h]
+                    + side_recv[s, :, part].astype(jnp.float32)
+                    + ring_sum[s, h].astype(jnp.float32)
+                ).astype(jnp.bfloat16)
+
+            sum_ring(s, h).start()
+
     def step(s, carry):
         @pl.when(s >= 1)
         def _():
-            for copy in tok_ring(s - 1):
-                copy.wait_recv()
+            gates_ring(s - 1).wait_recv()
 
         @pl.when(s < chips - 1)
         def _():
-            for copy in tok_ring(s):
-                copy.start()
-
-        for copy in tok_side(s, core):
-            copy.start()
+            gates_ring(s).start()
+
+        gates_side(s, core).start()
+        for kind in (1, 0):
+
+            @pl.when(s >= 1)
+            def _():
+                tok_ring(s - 1, kind).wait_recv()
+
+            @pl.when(s < chips - 1)
+            def _():
+                tok_ring(s, kind).start()
+
+            tok_side(s, kind, core).start()
 
         @pl.when(s == 0)
         def _():
+            acc_in[...] = jnp.zeros_like(acc_in)
+            acc_down[...] = jnp.zeros_like(acc_down)
             for load in loads[3:]:
                 load.wait()
 
-        for copy in tok_side(s, mate):
-            copy.wait_recv()
+        @pl.when(s >= lag + 1)
+        def _():
+            add_and_send(s - lag)
+
+        gates_side(s, mate).wait_recv()
+        tok_side(s, 1, mate).wait_recv()
+        tok_side(s, 0, mate).wait_recv()
 
         pick = (lax.broadcasted_iota(jnp.int32, (slots, lanes), 0) == chip).astype(jnp.bfloat16)
         for c in range(2):
@@ -393,34 +448,23 @@
         side_gate_send[s] = gate_rows[mate]
         for copy in sum_side(s):
             copy.start()
-        for copy in sum_side(s):
-            copy.wait_recv()
 
         @pl.when(s == 0)
         def _():
-            home[...] = dx_part[core] + side_recv[s].astype(jnp.float32)
-            home_gate[...] = gate_rows[core] + side_gate_recv[s]
-
-        @pl.when(s == 1)
-        def _():
-            ring_sum[s] = (dx_part[core] + side_recv[s].astype(jnp.float32)).astype(jnp.bfloat16)
-            ring_gate[s] = gate_rows[core] + side_gate_recv[s]
-
-        @pl.when(s >= 2)
-        def _():
-            for copy in sum_ring(s - 1):
-                copy.wait_recv()
-            ring_sum[s] = (
-                dx_part[core]
-                + side_recv[s].astype(jnp.float32)
-                + ring_sum[s].astype(jnp.float32)
-            ).astype(jnp.bfloat16)
-            ring_gate[s] = gate_rows[core] + side_gate_recv[s] + ring_gate[s]
+            for h in range(2):
+                home[h] = dx_part[core, :, h * half : (h + 1) * half]
+            home_gate[...] = gate_rows[core]
 
         @pl.when(s >= 1)
         def _():
-            for copy in sum_ring(s):
-                copy.start()
+            for h in range(2):
+                own_part[s % kept, h] = dx_part[core, :, h * half : (h + 1) * half]
+            own_gate[s % kept] = gate_rows[core]
+
+        @pl.when(s == chips - 1)
+        def _():
+            for late in range(lag - 1, 0, -1):
+                add_and_send(chips - 1 - late)
 
         @pl.loop(0, width // cols)
         def _(n):
@@ -445,6 +489,7 @@
         return carry
 
     lax.fori_loop(0, chips, step, 0)
+    add_and_send(chips - 1)
 
     for j in range(tiles):
         w_mat[j] = acc_in[j].astype(jnp.bfloat16)
@@ -461,10 +506,16 @@
     for store in stores:
         store.start()
 
-    for copy in sum_ring(chips - 1):
+    for copy in sum_side(0):
         copy.wait_recv()
-    dx_out[...] = (home[...] + ring_sum[chips].astype(jnp.float32)).astype(jnp.bfloat16)
-    home_gate[...] += ring_gate[chips]
+    gsum_ring(chips - 1).wait_recv()
+    home_gate[...] += side_gate_recv[0] + ring_gate[chips]
+    for h in range(2):
+        part = slice(h * half, (h + 1) * half)
+        sum_ring(chips - 1, h).wait_recv()
+        dx_out[:, part] = (
+            home[h] + side_recv[0, :, part].astype(jnp.float32) + ring_sum[chips, h].astype(jnp.float32)
+        ).astype(jnp.bfloat16)
     last = [
         pltpu.make_async_copy(dx_out, dx_hbm, load_sem.at[len(stores)]),
         pltpu.make_async_copy(home_gate, gg_hbm, load_sem.at[len(stores) + 1]),
@@ -475,16 +526,19 @@
     def drain(s, carry):
         @pl.when(s < chips - 1)
         def _():
-            for copy in tok_ring(s):
-                copy.wait_send()
+            gates_ring(s).wait_send()
+            for kind in range(2):
+                tok_ring(s, kind).wait_send()
 
         @pl.when(s >= 1)
         def _():
-            for copy in sum_ring(s):
-                copy.wait_send()
-
-        for copy in tok_side(s, core):
-            copy.wait_send()
+            gsum_ring(s).wait_send()
+            for h in range(2):
+                sum_ring(s, h).wait_send()
+
+        gates_side(s, core).wait_send()
+        for kind in range(2):
+            tok_side(s, kind, core).wait_send()
         for copy in sum_side(s):
             copy.wait_send()
         return carry
@@ -492,6 +546,12 @@
     lax.fori_loop(0, chips, drain, 0)
     for store in stores + last:
         store.wait()
+
+
+def hand_over(*refs):
+    count = len(refs) // 2
+    for source, target in zip(refs[:count], refs[count:]):
+        target[...] = source[...]
 
 
 def ring_local(x_rows, out_grad, expert_ids, gate_values, w_gate, w_up, w_down):
@@ -535,8 +595,10 @@
             pltpu.VMEM((2 * rows, lanes), f32),
             pltpu.VMEM((2 * rows, lanes), f32),
             pltpu.VMEM((2, rows, width), f32),
-            pltpu.VMEM((rows, width), f32),
-            pltpu.VMEM((chips + 1, rows, width), bf16),
+            pltpu.VMEM((2, rows, width // 2), f32),
+            pltpu.VMEM((3, 2, rows, width // 2), f32),
+            pltpu.VMEM((3, slots, rows), f32),
+            pltpu.VMEM((chips + 1, 2, rows, width // 2), bf16),
             pltpu.VMEM((chips, rows, width), bf16),
             pltpu.VMEM((chips, rows, width), bf16),
             pltpu.VMEM((chips + 1, slots, rows), f32),
@@ -547,7 +609,10 @@
             pltpu.VMEM((rows, width), bf16),
             dma((4 + 2 * tiles,)),
         ]
-        + [dma((chips + 1,))] * 16,
+        + [dma((chips + 1, 2))] * 4
+        + [dma((chips + 1,))] * 4
+        + [dma((chips + 1, 2))] * 2
+        + [dma((chips + 1,))] * 6,
         compiler_params=pltpu.CompilerParams(
             collective_id=0, has_side_effects=True, vmem_limit_bytes=60 * 2**20
         ),
@@ -555,6 +620,21 @@
             flops=flops, bytes_accessed=12 * width * hid, transcendentals=nodes * rows * hid
         ),
     )(x_rows, out_grad, gate_table, w_gate, w_up, w_down)
+    results = (x_grad, d_gate, d_up, d_down)
+    pieces = 4
+    blocks = [
+        pl.BlockSpec((rows // pieces, width), lambda i: (i, 0)),
+        pl.BlockSpec((1, width // pieces, hid), lambda i: (0, i, 0)),
+        pl.BlockSpec((1, width // pieces, hid), lambda i: (0, i, 0)),
+        pl.BlockSpec((1, hid // pieces, width), lambda i: (0, i, 0)),
+    ]
+    x_grad, d_gate, d_up, d_down = pl.pallas_call(
+        hand_over,
+        grid=(pieces,),
+        out_shape=tuple(jax.ShapeDtypeStruct(r.shape, r.dtype) for r in results),
+        in_specs=blocks,
+        out_specs=tuple(blocks),
+    )(*results)
     gate_grad = jnp.stack(
         [jnp.sum(jnp.where(chosen, gate_sum, 0.0), axis=0) for chosen in named], axis=1
     )

time: 149 us -> 139 us (0.933)
  local copies, waits for them, and re-layouts: 9.49 us -> 1.67 us
  Pallas kernels: 137 us -> 135 us
    unnamed x8 -> x0, local copies, waits for them, and re-layouts: 7.83 us -> none
    pallas_call x1, Pallas kernels: 137 us -> 130 us  [ring_local(): pl.pallas_call(functools.partial(ring_kernel, nodes), out_shape=(jax.Shap...]
    pallas_call x0 -> x1, Pallas kernels: none -> 5.28 us  [ring_local(): pl.pallas_call(hand_over, grid=(pieces,), out_shape=tuple((jax.ShapeDtype...]
where the time goes in v1:
time: 139 us
  Pallas kernels  135 us (97%)
  other arithmetic  1.91 us (1%)
  local copies, waits for them, and re-layouts  1.67 us (1%)
    pallas_call x1, Pallas kernels, ring_local(): pl.pallas_call(functools.partial(ring_kernel, nodes), out_shape=(jax.Shap...  130 us
    pallas_call x1, Pallas kernels, ring_local(): pl.pallas_call(hand_over, grid=(pieces,), out_shape=tuple((jax.ShapeDtype...  5.28 us

profile of v1, /device:TPU:0, one launch (start us, length us, event | category | flops | bytes accessed | tf_op | source)
XLA Modules:
  0.0 139.0 jit_solution(7496622490152432149)
XLA Ops:
  0.6 0.8 slice_bitcast_fusion.7
  1.5 0.8 slice_bitcast_fusion.6
  2.3 0.6 add_convert_fusion.gt_hbm
  2.9 129.5 %shard_map.110 = (bf16[128,2048]{1,0:T(8,128)(2,1)}, f32[16,128]{1,0:T(8,128)}, bf16[1,2048,384]{2,1,0:T(8,128)(2,1)}, bf16[1,2048,384]{2,1,0:T(8,128)(2,1)}, bf16[1,384,2048]{2,1,0:T(8,128)(2,1)}) custom-call(bf16[128,2048]{1,0:T(8,128)(2,1)} %x_hbm.1, bf16[128,2048]{1,0:T(8,128)(2,1)} %g_hbm.1, bf16[16,128]{1,0:T(8,128)(2,1)} %add_convert_fusion.gt_hbm, ...), custom_call_target="tpu_custom_call" | custom-call | flops 25769803776 | bytes 9437184 | tf_op jit(solution)/shard_map/pallas_call | solution.py:574
  132.4 0.7 select_reduce_fusion.3
  133.1 0.6 pad_maximum_fusion
  133.7 5.3 %shard_map.111 = (bf16[128,2048]{1,0:T(8,128)(2,1)}, bf16[1,2048,384]{2,1,0:T(8,128)(2,1)}, bf16[1,2048,384]{2,1,0:T(8,128)(2,1)}, bf16[1,384,2048]{2,1,0:T(8,128)(2,1)}) custom-call(bf16[128,2048]{1,0:T(8,128)(2,1)} %get-tuple-element.14.refs_0_, bf16[1,2048,384]{2,1,0:T(8,128)(2,1)} %get-tuple-element.15.refs_1_, ...), custom_call_target="tpu_custom_call" | custom-call | tf_op jit(solution)/shard_map/pallas_call | solution.py:631

commit v2 on v1

--- a/solution.py
+++ b/solution.py
@@ -132,12 +132,13 @@
     nodes,
     x_hbm,
     g_hbm,
-    gt_hbm,
+    ids_ref,
+    values_ref,
     wg_hbm,
     wu_hbm,
     wd_hbm,
     dx_hbm,
-    gg_hbm,
+    gg_ref,
     dwg_hbm,
     dwu_hbm,
     dwd_hbm,
@@ -153,6 +154,10 @@
     gate_col,
     gate_part,
     dx_part,
+    pack_send,
+    pack_recv,
+    sum_pack_send,
+    sum_pack_recv,
     home,
     own_part,
     own_gate,
@@ -206,11 +211,12 @@
     ahead = {"node": node_at(place + step_dir)}
     behind = {"node": node_at(place - step_dir)}
     other = {"node": chip * 2 + mate}
+    chip_ahead = node_at(place + step_dir) // 2
+    chip_behind = node_at(place - step_dir) // 2
 
     loads = [
         (x_hbm, tok.at[0, 0, core]),
         (g_hbm, tok.at[0, 1, core]),
-        (gt_hbm, gates.at[0, core]),
         (wd_hbm.at[0], wd_mat),
     ]
     for j in range(tiles):
@@ -221,7 +227,7 @@
         pltpu.make_async_copy(source, target, load_sem.at[i])
         for i, (source, target) in enumerate(loads)
     ]
-    for load in loads:
+    for load in loads[:2]:
         load.start()
 
     barrier = pltpu.get_barrier_semaphore()
@@ -245,6 +251,49 @@
             tok.at[s + 1, kind, core],
             tok_ring_send.at[s, kind],
             tok_ring_recv.at[s + 1, kind],
+            ahead,
+        )
+
+    limit = pack_send.shape[1]
+
+    def select(table, expert):
+        named = lax.broadcasted_iota(jnp.int32, (slots, rows), 0) == expert
+        routed = jnp.where(named, table.astype(jnp.float32), 0.0) > 0.0
+        mask = jnp.max(routed.astype(jnp.float32), axis=0, keepdims=True)
+        before = lax.broadcasted_iota(jnp.int32, (rows, rows), 0) < lax.broadcasted_iota(
+            jnp.int32, (rows, rows), 1
+        )
+        rank = jnp.dot(
+            jnp.broadcast_to(mask, (slots, rows)).astype(jnp.bfloat16),
+            before.astype(jnp.bfloat16),
+            preferred_element_type=jnp.float32,
+        )[:1]
+        place_of = lax.broadcasted_iota(jnp.int32, (limit, rows), 0).astype(jnp.float32)
+        return jnp.where(place_of == rank, mask, 0.0).astype(jnp.bfloat16)
+
+    def packed(chooser, dense):
+        return jnp.dot(chooser, dense, preferred_element_type=jnp.float32).astype(jnp.bfloat16)
+
+    def spread(chooser, rows_packed):
+        return lax.dot_general(
+            chooser, rows_packed, (((0,), (0,)), ((), ())), preferred_element_type=jnp.float32
+        )
+
+    def tok_pack(kind):
+        return remote(
+            pack_send.at[kind],
+            pack_recv.at[kind],
+            tok_ring_send.at[chips - 2, kind],
+            tok_ring_recv.at[chips - 1, kind],
+            ahead,
+        )
+
+    def sum_pack(h):
+        return remote(
+            sum_pack_send.at[h],
+            sum_pack_recv.at[h],
+            sum_ring_send.at[1, h],
+            sum_ring_recv.at[2, h],
             ahead,
         )
 
@@ -309,12 +358,20 @@
             ),
         )
 
-    for load in loads[:3]:
+    slots = gates.shape[2]
+    top = ids_ref.shape[0]
+    expert = lax.broadcasted_iota(jnp.int32, (slots, rows), 0)
+    ids, values = ids_ref[...], values_ref[...]
+    table = jnp.zeros((slots, rows), jnp.float32)
+    for k in range(top):
+        table = table + jnp.where(ids[k : k + 1] == expert, values[k : k + 1], 0.0)
+    gates[0, core] = table.astype(jnp.bfloat16)
+
+    for load in loads[:2]:
         load.wait()
 
     contract_last = (((1,), (1,)), ((), ()))
     contract_first = (((0,), (0,)), ((), ()))
-    slots = gates.shape[2]
 
     lag = 2
     kept = own_part.shape[0]
@@ -339,11 +396,22 @@
 
             @pl.when(s == 1)
             def _():
+                total = own_part[s % kept, h] + side_recv[s, :, part].astype(jnp.float32)
+                chooser = select(gates[s, core], chip)
+                sum_pack_send[h] = packed(chooser, total.astype(jnp.bfloat16))
+                sum_pack(h).start()
+
+            @pl.when(s == 2)
+            def _():
+                sum_pack(h).wait_recv()
+                chooser = select(gates[s, core], chip_behind)
                 ring_sum[s, h] = (
-                    own_part[s % kept, h] + side_recv[s, :, part].astype(jnp.float32)
+                    own_part[s % kept, h]
+                    + side_recv[s, :, part].astype(jnp.float32)
+                    + spread(chooser, sum_pack_recv[h])
                 ).astype(jnp.bfloat16)
 
-            @pl.when(s >= 2)
+            @pl.when(s >= 3)
             def _():
                 sum_ring(s - 1, h).wait_recv()
                 ring_sum[s, h] = (
@@ -352,7 +420,9 @@
                     + ring_sum[s, h].astype(jnp.float32)
                 ).astype(jnp.bfloat16)
 
-            sum_ring(s, h).start()
+            @pl.when(s >= 2)
+            def _():
+                sum_ring(s, h).start()
 
     def step(s, carry):
         @pl.when(s >= 1)
@@ -366,21 +436,35 @@
         gates_side(s, core).start()
         for kind in (1, 0):
 
-            @pl.when(s >= 1)
+            @pl.when((s >= 1) & (s < chips - 1))
             def _():
                 tok_ring(s - 1, kind).wait_recv()
 
-            @pl.when(s < chips - 1)
+            @pl.when(s < chips - 2)
             def _():
                 tok_ring(s, kind).start()
 
+            @pl.when(s == chips - 2)
+            def _():
+                chooser = select(gates[s, core], chip_ahead)
+                pack_send[kind] = packed(chooser, tok[s, kind, core])
+                tok_pack(kind).start()
+
+            @pl.when(s == chips - 1)
+            def _():
+                tok_pack(kind).wait_recv()
+                chooser = select(gates[s, core], chip)
+                tok[s, kind, core] = spread(chooser, pack_recv[kind]).astype(jnp.bfloat16)
+
             tok_side(s, kind, core).start()
 
         @pl.when(s == 0)
         def _():
+            for load in loads[2:]:
+                load.start()
             acc_in[...] = jnp.zeros_like(acc_in)
             acc_down[...] = jnp.zeros_like(acc_down)
-            for load in loads[3:]:
+            for load in loads[2:]:
                 load.wait()
 
         @pl.when(s >= lag + 1)
@@ -509,7 +593,10 @@
     for copy in sum_side(0):
         copy.wait_recv()
     gsum_ring(chips - 1).wait_recv()
-    home_gate[...] += side_gate_recv[0] + ring_gate[chips]
+    gate_sums = home_gate[...] + side_gate_recv[0] + ring_gate[chips]
+    for k in range(top):
+        chosen = jnp.where(ids[k : k + 1] == expert, gate_sums, 0.0)
+        gg_ref[k : k + 1, :] = jnp.sum(chosen, axis=0, keepdims=True)
     for h in range(2):
         part = slice(h * half, (h + 1) * half)
         sum_ring(chips - 1, h).wait_recv()
@@ -518,7 +605,6 @@
         ).astype(jnp.bfloat16)
     last = [
         pltpu.make_async_copy(dx_out, dx_hbm, load_sem.at[len(stores)]),
-        pltpu.make_async_copy(home_gate, gg_hbm, load_sem.at[len(stores) + 1]),
     ]
     for store in last:
         store.start()
@@ -527,14 +613,28 @@
         @pl.when(s < chips - 1)
         def _():
             gates_ring(s).wait_send()
-            for kind in range(2):
+
+        @pl.when(s >= 1)
+        def _():
+            gsum_ring(s).wait_send()
+
+        for kind in range(2):
+
+            @pl.when(s < chips - 2)
+            def _():
                 tok_ring(s, kind).wait_send()
 
-        @pl.when(s >= 1)
-        def _():
-            gsum_ring(s).wait_send()
-            for h in range(2):
-                sum_ring(s, h).wait_send()
+            @pl.when(s == chips - 2)
+            def _():
+                tok_pack(kind).wait_send()
+
+            @pl.when(s == 1)
+            def _():
+                sum_pack(kind).wait_send()
+
+            @pl.when(s >= 2)
+            def _():
+                sum_ring(s, kind).wait_send()
 
         gates_side(s, core).wait_send()
         for kind in range(2):
@@ -562,26 +662,25 @@
     lanes = 128
     tiles = hid // lanes
     slots = (chips + 15) // 16 * 16
-    expert = jnp.arange(slots, dtype=jnp.int32)[:, None]
-    named = [expert == expert_ids[:, k][None, :] for k in range(expert_ids.shape[1])]
-    gate_table = sum(
-        jnp.where(named[k], gate_values[:, k][None, :], 0.0) for k in range(len(named))
-    ).astype(jnp.bfloat16)
+    capacity = 2 * max(1, 5 * rows * expert_ids.shape[1] // (8 * chips))
+    limit = min(rows, (capacity + 15) // 16 * 16)
+    top = expert_ids.shape[1]
     any_space = pl.BlockSpec(memory_space=pl.ANY)
+    vmem_space = pl.BlockSpec(memory_space=pltpu.VMEM)
     bf16, f32 = jnp.bfloat16, jnp.float32
     dma = pltpu.SemaphoreType.DMA
     flops = 2 * nodes * rows * width * hid * 8
-    x_grad, gate_sum, d_gate, d_up, d_down = pl.pallas_call(
+    results = pl.pallas_call(
         functools.partial(ring_kernel, nodes),
         out_shape=(
             jax.ShapeDtypeStruct((rows, width), bf16),
-            jax.ShapeDtypeStruct((slots, rows), f32),
+            jax.ShapeDtypeStruct((top, rows), f32),
             jax.ShapeDtypeStruct((1, width, hid), bf16),
             jax.ShapeDtypeStruct((1, width, hid), bf16),
             jax.ShapeDtypeStruct((1, hid, width), bf16),
         ),
-        in_specs=[any_space] * 6,
-        out_specs=(any_space,) * 5,
+        in_specs=[any_space] * 2 + [vmem_space] * 2 + [any_space] * 3,
+        out_specs=(any_space, vmem_space) + (any_space,) * 3,
         scratch_shapes=[
             pltpu.VMEM((chips, 2, 2, rows, width), bf16),
             pltpu.VMEM((chips, 2, slots, rows), bf16),
@@ -595,6 +694,10 @@
             pltpu.VMEM((2 * rows, lanes), f32),
             pltpu.VMEM((2 * rows, lanes), f32),
             pltpu.VMEM((2, rows, width), f32),
+            pltpu.VMEM((2, limit, width), bf16),
+            pltpu.VMEM((2, limit, width), bf16),
+            pltpu.VMEM((2, limit, width // 2), bf16),
+            pltpu.VMEM((2, limit, width // 2), bf16),
             pltpu.VMEM((2, rows, width // 2), f32),
             pltpu.VMEM((3, 2, rows, width // 2), f32),
             pltpu.VMEM((3, slots, rows), f32),
@@ -619,26 +722,23 @@
         cost_estimate=pl.CostEstimate(
             flops=flops, bytes_accessed=12 * width * hid, transcendentals=nodes * rows * hid
         ),
-    )(x_rows, out_grad, gate_table, w_gate, w_up, w_down)
-    results = (x_grad, d_gate, d_up, d_down)
+    )(x_rows, out_grad, expert_ids.T, gate_values.T, w_gate, w_up, w_down)
     pieces = 4
     blocks = [
         pl.BlockSpec((rows // pieces, width), lambda i: (i, 0)),
+        pl.BlockSpec((top, rows), lambda i: (0, 0)),
         pl.BlockSpec((1, width // pieces, hid), lambda i: (0, i, 0)),
         pl.BlockSpec((1, width // pieces, hid), lambda i: (0, i, 0)),
         pl.BlockSpec((1, hid // pieces, width), lambda i: (0, i, 0)),
     ]
-    x_grad, d_gate, d_up, d_down = pl.pallas_call(
+    x_grad, gate_grad, d_gate, d_up, d_down = pl.pallas_call(
         hand_over,
         grid=(pieces,),
         out_shape=tuple(jax.ShapeDtypeStruct(r.shape, r.dtype) for r in results),
         in_specs=blocks,
         out_specs=tuple(blocks),
     )(*results)
-    gate_grad = jnp.stack(
-        [jnp.sum(jnp.where(chosen, gate_sum, 0.0), axis=0) for chosen in named], axis=1
-    )
-    return (x_grad, gate_grad, d_gate, d_up, d_down)
+    return (x_grad, gate_grad.T, d_gate, d_up, d_down)
 
 
 def solution(mesh):

time: 139 us -> 131 us (0.942)
  Pallas kernels: 135 us -> 130 us
  other arithmetic: 1.91 us -> 0 us
  local copies, waits for them, and re-layouts: 1.67 us -> 0 us
    pallas_call x1, Pallas kernels: 130 us -> 124 us  [ring_local(): pl.pallas_call(functools.partial(ring_kernel, nodes), out_shape=(jax.Shap...]
where the time goes in v2:
time: 131 us; the launch traced here: 130 us
  Pallas kernels  130 us (99%)
    pallas_call x1, Pallas kernels, ring_local(): pl.pallas_call(functools.partial(ring_kernel, nodes), out_shape=(jax.Shap...  124 us
    pallas_call x1, Pallas kernels, ring_local(): pl.pallas_call(hand_over, grid=(pieces,), out_shape=tuple((jax.ShapeDtype...  5.3 us

profile of v2, /device:TPU:0, one launch (start us, length us, event | category | flops | bytes accessed | tf_op | source)
XLA Modules:
  0.0 130.4 jit_solution(15711609081739229994)
XLA Ops:
  0.6 124.5 %shard_map.110 = (bf16[128,2048]{1,0:T(8,128)(2,1)}, f32[4,128]{1,0:T(4,128)}, bf16[1,2048,384]{2,1,0:T(8,128)(2,1)}, bf16[1,2048,384]{2,1,0:T(8,128)(2,1)}, bf16[1,384,2048]{2,1,0:T(8,128)(2,1)}) custom-call(bf16[128,2048]{1,0:T(8,128)(2,1)} %x_hbm.1, bf16[128,2048]{1,0:T(8,128)(2,1)} %g_hbm.1, s32[4,128]{1,0:T(4,128)} %bitcast.3, f32[4,128]{1,0:T(4,128)} %bitcast.4, ...), custom_call_target="tpu_custom_call" | custom-call | flops 25769803776 | bytes 9437184 | tf_op jit(solution)/shard_map/pallas_call | solution.py:673
  125.1 5.3 %shard_map.111 = (bf16[128,2048]{1,0:T(8,128)(2,1)}, f32[4,128]{1,0:T(4,128)}, bf16[1,2048,384]{2,1,0:T(8,128)(2,1)}, bf16[1,2048,384]{2,1,0:T(8,128)(2,1)}, bf16[1,384,2048]{2,1,0:T(8,128)(2,1)}) custom-call(bf16[128,2048]{1,0:T(8,128)(2,1)} %get-tuple-element.15.refs_0_, f32[4,128]{1,0:T(4,128)} %get-tuple-element.16.refs_1_, ...), custom_call_target="tpu_custom_call" | custom-call | tf_op jit(solution)/shard_map/pallas_call | solution.py:734

commit v3 on v2

--- a/solution.py
+++ b/solution.py
@@ -723,7 +723,7 @@
             flops=flops, bytes_accessed=12 * width * hid, transcendentals=nodes * rows * hid
         ),
     )(x_rows, out_grad, expert_ids.T, gate_values.T, w_gate, w_up, w_down)
-    pieces = 4
+    pieces = 2
     blocks = [
         pl.BlockSpec((rows // pieces, width), lambda i: (i, 0)),
         pl.BlockSpec((top, rows), lambda i: (0, 0)),

time: 131 us -> 130 us (level)
  no operation moved by 1% of the time
where the time goes in v3:
time: 130 us; the launch traced here: 129 us
  Pallas kernels  129 us (99%)
    pallas_call x1, Pallas kernels, ring_local(): pl.pallas_call(functools.partial(ring_kernel, nodes), out_shape=(jax.Shap...  124 us
    pallas_call x1, Pallas kernels, ring_local(): pl.pallas_call(hand_over, grid=(pieces,), out_shape=tuple((jax.ShapeDtype...  4.28 us

profile of v3, /device:TPU:0, one launch (start us, length us, event | category | flops | bytes accessed | tf_op | source)
XLA Modules:
  0.0 129.4 jit_solution(1841018838217503589)
XLA Ops:
  0.6 124.5 %shard_map.110 = (bf16[128,2048]{1,0:T(8,128)(2,1)}, f32[4,128]{1,0:T(4,128)}, bf16[1,2048,384]{2,1,0:T(8,128)(2,1)}, bf16[1,2048,384]{2,1,0:T(8,128)(2,1)}, bf16[1,384,2048]{2,1,0:T(8,128)(2,1)}) custom-call(bf16[128,2048]{1,0:T(8,128)(2,1)} %x_hbm.1, bf16[128,2048]{1,0:T(8,128)(2,1)} %g_hbm.1, s32[4,128]{1,0:T(4,128)} %bitcast.3, f32[4,128]{1,0:T(4,128)} %bitcast.4, ...), custom_call_target="tpu_custom_call" | custom-call | flops 25769803776 | bytes 9437184 | tf_op jit(solution)/shard_map/pallas_call | solution.py:673
  125.1 4.3 %shard_map.111 = (bf16[128,2048]{1,0:T(8,128)(2,1)}, f32[4,128]{1,0:T(4,128)}, bf16[1,2048,384]{2,1,0:T(8,128)(2,1)}, bf16[1,2048,384]{2,1,0:T(8,128)(2,1)}, bf16[1,384,2048]{2,1,0:T(8,128)(2,1)}) custom-call(bf16[128,2048]{1,0:T(8,128)(2,1)} %get-tuple-element.15.refs_0_, f32[4,128]{1,0:T(4,128)} %get-tuple-element.16.refs_1_, ...), custom_call_target="tpu_custom_call" | custom-call | tf_op jit(solution)/shard_map/pallas_call | solution.py:734
